TPU v7x, 32 devices: a whole 2x2x4 slice. The times are simulated.
32 devices in a mesh: gx: 2 (over core), gy: 4 (over y, x), gz: 4 (over z).
Axes of the slice: x: 2, y: 2, z: 4, core: 2. Of those that a mesh axis runs over, the one named last changes fastest.
Arguments:
- displacement: float32 [3, 16, 64, 512], P(None, 'gx', 'gy', 'gz'), may hold values from -6 to 6
- adjoint_load: float32 [3, 16, 64, 512], P(None, 'gx', 'gy', 'gz'), may hold values from -6 to 6
- bone_mask: int32 [16, 64, 512], P('gx', 'gy', 'gz'), may hold values 0 or 1
- elem_zone: int32 [16, 64, 512], P('gx', 'gy', 'gz'), may hold values from 0 to 127, as said below
- zone_slot: int32 [128], replicated, may hold values from 0 to 127, each once
- zone_modulus: float32 [128], P(('gx', 'gy', 'gz')), may hold values from 0.5 to 4
Outputs:
- adjoint: float32 [3, 16, 64, 512], P(None, 'gx', 'gy', 'gz')
- zone_gradient: float32 [128], P(('gx', 'gy', 'gz'))
Inputs may be any that keep to these rules, and one draw needn't show every extreme that they name: `elem_zone`: zones are cubes of 16 voxels on a grid shifted by a drawn offset that wraps cyclically, so a cube cut by one end of the window continues at the other end under the same number; zones are numbered in a drawn order and every zone number occurs. `zone_slot`: each zone appears at exactly one position.
All inputs are finite; a program needn't handle non-finite values. No bound on the sum of `bone_mask` on one device may be relied on, other than what follows from the above.
Results may differ from a plain program's by a relative error of at most 0.0003.
Values sent between devices are 32-bit elements; how exact they have to be, the bound alone decides.
A program may use at most 64 MiB of HBM per device.

v0:
```python
import jax
import jax.numpy as jnp
import numpy as np
from jax import lax
from jax.sharding import PartitionSpec as P

ZS = 16


spring_rate = 0.1


def with_halo(value, sides, width):
    for axis, dim in sides:
        devices, length = (lax.axis_size(axis), value.shape[dim])
        up = [(i, (i + 1) % devices) for i in range(devices - 1)]
        down = [(j, i) for i, j in up]
        last = lax.slice_in_dim(value, length - width, length, axis=dim)
        leading = lax.slice_in_dim(value, 0, width, axis=dim)
        before = lax.ppermute(last, axis, up)
        after = lax.ppermute(leading, axis, down)
        value = jnp.concatenate([before, value, after], axis=dim)
    return value


def hex_stiffness():
    poisson = 0.3
    lame_first = poisson / ((1.0 + poisson) * (1.0 - 2.0 * poisson))
    shear_mod = 0.5 / (1.0 + poisson)
    elastic = np.zeros((6, 6))
    elastic[:3, :3] = lame_first
    for index in range(3):
        elastic[index, index] += 2.0 * shear_mod
        elastic[index + 3, index + 3] = shear_mod
    corner_signs = np.array(
        [
            [2.0 * (corner // 4) - 1.0, 2.0 * (corner // 2 % 2) - 1.0, 2.0 * (corner % 2) - 1.0]
            for corner in range(8)
        ]
    )
    gauss_value = 1.0 / np.sqrt(3.0)
    stiffness = np.zeros((24, 24))
    for gauss_x in (-gauss_value, gauss_value):
        for gauss_y in (-gauss_value, gauss_value):
            for gauss_z in (-gauss_value, gauss_value):
                where_at = np.array([gauss_x, gauss_y, gauss_z])
                strain_map = np.zeros((6, 24))
                for corner in range(8):
                    factor = 1.0 + corner_signs[corner] * where_at
                    grad_x = corner_signs[corner, 0] * factor[1] * factor[2] / 4.0
                    grad_y = corner_signs[corner, 1] * factor[0] * factor[2] / 4.0
                    grad_z = corner_signs[corner, 2] * factor[0] * factor[1] / 4.0
                    column = 3 * corner
                    strain_map[0, column] = grad_x
                    strain_map[1, column + 1] = grad_y
                    strain_map[2, column + 2] = grad_z
                    strain_map[3, column] = grad_y
                    strain_map[3, column + 1] = grad_x
                    strain_map[4, column + 1] = grad_z
                    strain_map[4, column + 2] = grad_y
                    strain_map[5, column] = grad_z
                    strain_map[5, column + 2] = grad_x
                stiffness += strain_map.T @ elastic @ strain_map / 8.0
    return stiffness


def corner_stack(field_in):
    rows_x = field_in.shape[1] - 1
    rows_y = field_in.shape[2] - 1
    rows_z = field_in.shape[3] - 1
    pieces = []
    for corner in range(8):
        shift_x, shift_y, shift_z = (corner // 4, corner // 2 % 2, corner % 2)
        pieces.append(
            field_in[
                :,
                shift_x : shift_x + rows_x,
                shift_y : shift_y + rows_y,
                shift_z : shift_z + rows_z,
            ]
        )
    return jnp.concatenate(pieces, axis=0)


def apply_local(field_in, moduli, stiffness):
    rows_x = field_in.shape[1] - 1
    rows_y = field_in.shape[2] - 1
    rows_z = field_in.shape[3] - 1
    stacked = corner_stack(field_in)
    forces = (
        jnp.einsum("ij,jxyz->ixyz", stiffness, stacked, precision=lax.Precision.HIGHEST)
        * moduli[None]
    )
    result = spring_rate * field_in[:, 1:-1, 1:-1, 1:-1]
    for corner in range(8):
        shift_x, shift_y, shift_z = (corner // 4, corner // 2 % 2, corner % 2)
        result = (
            result
            + forces[
                3 * corner : 3 * corner + 3,
                1 - shift_x : 1 - shift_x + rows_x - 1,
                1 - shift_y : 1 - shift_y + rows_y - 1,
                1 - shift_z : 1 - shift_z + rows_z - 1,
            ]
        )
    return result


def element_terms(adjoint_nodes, disp_nodes, bone_float, stiffness):
    stacked_disp = corner_stack(disp_nodes)
    stacked_adj = corner_stack(adjoint_nodes)
    forces = jnp.einsum("ij,jxyz->ixyz", stiffness, stacked_disp, precision=lax.Precision.HIGHEST)
    return -(ZS ** (-1.5)) * jnp.sum(stacked_adj * forces, axis=0) * bone_float


def edge_mask(position, extent, count):
    places = jnp.arange(count + 2, dtype=jnp.int32) - 1 + position * count
    return ((places >= 0) & (places < extent * count)).astype(jnp.float32)


def on_device(displacement, adjoint_load, bone_mask, elem_zone, zone_slot, zone_modulus):
    stiffness = jnp.asarray(hex_stiffness(), dtype=jnp.float32)
    bone_float = bone_mask.astype(jnp.float32)
    slot_map = jnp.take(zone_slot, elem_zone)
    all_moduli = lax.all_gather(zone_modulus, ("gx", "gy", "gz"), axis=0, tiled=True)
    moduli = jnp.take(all_moduli, slot_map) * bone_float
    fixed_fields = jnp.concatenate([displacement, moduli[None]], axis=0)
    count_x, count_y, count_z = moduli.shape
    zone_count = zone_slot.shape[0]
    fixed_wide = with_halo(fixed_fields, (("gx", 1), ("gy", 2), ("gz", 3)), 2)
    disp_nodes = fixed_wide[0:3, 2 : count_x + 3, 2 : count_y + 3, 2 : count_z + 3]
    outer_moduli = fixed_wide[3, : count_x + 3, : count_y + 3, : count_z + 3]
    inner_moduli = fixed_wide[3, 1 : count_x + 2, 1 : count_y + 2, 1 : count_z + 2]
    load_wide = with_halo(adjoint_load, (("gx", 1), ("gy", 2), ("gz", 3)), 2)
    valid_x = edge_mask(lax.axis_index("gx"), lax.axis_size("gx"), count_x)
    valid_y = edge_mask(lax.axis_index("gy"), lax.axis_size("gy"), count_y)
    valid_z = edge_mask(lax.axis_index("gz"), lax.axis_size("gz"), count_z)
    validity = valid_x[:, None, None] * valid_y[None, :, None] * valid_z[None, None, :]
    krylov = apply_local(load_wide, outer_moduli, stiffness) * validity[None]
    krylov_applied = apply_local(krylov, inner_moduli, stiffness)
    krylov_own = krylov[:, 1 : count_x + 1, 1 : count_y + 1, 1 : count_z + 1]
    load_norm, cross_term, krylov_norm, krylov_energy = lax.psum(
        (
            jnp.sum(adjoint_load * adjoint_load),
            jnp.sum(adjoint_load * krylov_own),
            jnp.sum(krylov_own * krylov_own),
            jnp.sum(krylov_own * krylov_applied),
        ),
        ("gx", "gy", "gz"),
    )
    determinant = cross_term * krylov_energy - krylov_norm * krylov_norm
    coef_load = (load_norm * krylov_energy - cross_term * krylov_norm) / determinant
    coef_krylov = (cross_term * cross_term - krylov_norm * load_norm) / determinant
    adjoint_nodes = (
        coef_load * load_wide[:, 2 : count_x + 3, 2 : count_y + 3, 2 : count_z + 3]
        + coef_krylov * krylov[:, 1 : count_x + 2, 1 : count_y + 2, 1 : count_z + 2]
    )
    adjoint = adjoint_nodes[:, :count_x, :count_y, :count_z]
    terms = element_terms(adjoint_nodes, disp_nodes, bone_float, stiffness)
    partial_sums = jax.ops.segment_sum(terms.ravel(), slot_map.ravel(), num_segments=zone_count)
    zone_gradient = lax.psum_scatter(
        partial_sums, ("gx", "gy", "gz"), scatter_dimension=0, tiled=True
    )
    return (adjoint, zone_gradient)


def solution(mesh):
    in_specs = (
        P(None, "gx", "gy", "gz"),
        P(None, "gx", "gy", "gz"),
        P("gx", "gy", "gz"),
        P("gx", "gy", "gz"),
        P(),
        P(("gx", "gy", "gz")),
    )
    out_specs = (P(None, "gx", "gy", "gz"), P(("gx", "gy", "gz")))
    return jax.shard_map(
        on_device, mesh=mesh, in_specs=in_specs, out_specs=out_specs, check_vma=False
    )
```

profile of v0, /device:TPU:0, one launch (start us, length us, event | category | flops | bytes accessed | tf_op | source)
XLA Modules:
  0.0 653.3 jit_solution(4751685476374561647)
XLA Ops:
  0.6 0.0 copy-start
  0.6 0.8 fusion.17
  1.5 2.4 collective-permute-start
  3.9 1.3 collective-permute-start.1
  5.2 0.9 dynamic-update-slice
  6.1 41.4 %all-reduce = f32[128]{0:T(128)S(1)} all-reduce(f32[128]{0:T(128)S(1)} %dynamic-update-slice), channel_id=1, replica_groups=mesh['gx'=2,'gy'=4,'gz'=4] {'gx','gy','gz'}, use_global_device_ids=true, to_apply=%add | all-reduce | flops 128 | bytes 1024
  47.5 0.8 compare_select_fusion.1
  48.3 0.0 copy-start.15
  48.4 0.0 copy-start.17
  48.4 97.2 %gather_fusion = s32[16384]{0:T(1024)S(1)} fusion(s32[128]{0:T(128)S(1)} %copy-done, s32[16384]{0:T(1024)S(1)} %broadcast_clamp_fusion.1), kind=kCustom, calls=%fused_computation | custom fusion | bytes 196608 | tf_op jit(solution)/shard_map/jit(_take)/gather | solution.py:124
  145.7 0.1 copy.26
  145.8 0.0 copy-start.13
  145.8 97.2 %gather_fusion.1 = f32[16384]{0:T(1024)S(1)} fusion(f32[128]{0:T(128)S(1)} %all-reduce, s32[16384]{0:T(1024)S(1)} %broadcast_clamp_fusion), kind=kCustom, calls=%fused_computation.1 | custom fusion | bytes 196608 | tf_op jit(solution)/shard_map/jit(_take)/gather | solution.py:126
  243.1 0.1 pad_maximum_fusion.22
  243.2 1.3 collective-permute-start.7
  244.5 3.0 collective-permute-start.6
  247.6 0.1 broadcast_multiply_fusion.1
  247.6 0.8 broadcast_multiply_fusion
  248.4 0.7 multiply_reduce_fusion.3
  249.1 0.2 constant_dynamic-update-slice_fusion.1
  249.4 1.3 collective-permute-start.3
  250.7 4.8 collective-permute-start.2
  255.5 0.7 pad_maximum_fusion.26
  256.2 1.3 collective-permute-start.9
  257.5 5.4 collective-permute-start.8
  263.0 0.1 pad_maximum_fusion.5
  263.1 0.3 fusion.13
  263.4 1.3 collective-permute-start.5
  264.7 4.6 collective-permute-start.4
  269.3 0.8 pad_maximum_fusion.8
  270.1 6.9 %collective-permute-done.5 = f32[3,12,20,2]{3,0,2,1:T(4,128)S(1)} collective-permute-done((f32[3,12,20,2]{3,0,2,1:T(4,128)S(1)}, f32[3,12,20,2]{3,0,2,1:T(4,128)S(1)}, u32[]{:S(2)}, u32[]{:S(2)}) %collective-permute-start.5) | collective-permute-done | bytes 5792 | tf_op jit(solution)/shard_map/ppermute | solution.py:21
  277.0 1.2 collective-permute-done.4
  278.2 0.8 pad_maximum_fusion
  279.0 4.7 fusion.10
  283.7 60.6 %concatenate.52 = f32[24,11,19,131]{3,0,2,1:T(8,128)} concatenate(f32[3,11,19,131]{3,0,2,1:T(4,128)} %get-tuple-element.28, f32[3,11,19,131]{3,0,2,1:T(4,128)} %get-tuple-element.27, f32[3,11,19,131]{3,0,2,1:T(4,128)} %get-tuple-element.26, f32[3,11,19,131]{3,0,2,1:T(4,128)} %get-tuple-element.25, f32[3,11,19,131]{3,0,2,1:T(4,128)} %get-tuple-element.24, ...), dimensions={0} | concatenate | bytes 5256768 | tf_op jit(solution)/shard_map/concatenate | solution.py:82
  344.3 0.2 pad_maximum_fusion.6
  344.5 0.0 copy-start.18
  344.5 0.3 fusion.14
  344.8 4.7 collective-permute-start.10
  349.5 1.5 collective-permute-start.11
  351.0 0.2 pad_maximum_fusion.7
  351.2 0.9 fusion.15
  352.1 5.3 collective-permute-done.10
  357.5 0.8 pad_maximum_fusion.15
  358.3 3.3 collective-permute-done.11
  361.6 1.0 pad_maximum_fusion.10
  362.7 5.0 multiply_bitcast_fusion
  367.7 2.1 fusion
  369.8 3.2 fusion.11
  373.0 42.4 %concatenate.57 = f32[24,9,17,129]{3,0,2,1:T(8,128)} concatenate(f32[3,9,17,129]{3,0,2,1:T(4,128)} %get-tuple-element.36, f32[3,9,17,129]{3,0,2,1:T(4,128)} %get-tuple-element.35, f32[3,9,17,129]{3,0,2,1:T(4,128)} %get-tuple-element.34, f32[3,9,17,129]{3,0,2,1:T(4,128)} %get-tuple-element.33, f32[3,9,17,129]{3,0,2,1:T(4,128)} %get-tuple-element.32, ...), dimensions={0} | concatenate | bytes 3789504 | tf_op jit(solution)/shard_map/concatenate | solution.py:82
  415.4 5.7 multiply_bitcast_fusion.1
  421.1 1.5 fusion.4
  422.6 40.0 %all-reduce.2 = (f32[]{:T(128)}, f32[]{:T(128)}, f32[]{:T(128)}, f32[]{:T(128)}) all-reduce(f32[]{:T(128)} %get-tuple-element.9, f32[]{:T(128)} %get-tuple-element.10, f32[]{:T(128)} %multiply_reduce_fusion.3, f32[]{:T(128)} %get-tuple-element.8), channel_id=1, replica_groups=mesh['gx'=2,'gy'=4,'gz'=4] {'gx','gy','gz'}, use_global_device_ids=true, to_apply=%region_5.6 | all-reduce | flops 4 | bytes 32 | tf_op jit(solution)/shard_map/psum | solution.py:142
  470.2 0.4 fusion.2
  470.6 1.7 fusion.12
  472.3 0.7 copy.29
  473.0 0.3 pad_maximum_fusion.1
  473.3 1.6 fusion.9
  474.9 10.5 %concatenate.60 = f32[24,8,16,128]{3,0,2,1:T(8,128)S(1)} concatenate(f32[3,8,16,128]{3,0,2,1:T(4,128)S(1)} %get-tuple-element.44, f32[3,8,16,128]{3,0,2,1:T(4,128)} %get-tuple-element.43, f32[3,8,16,128]{3,0,2,1:T(4,128)} %get-tuple-element.42, f32[3,8,16,128]{3,0,2,1:T(4,128)} %get-tuple-element.41, f32[3,8,16,128]{3,0,2,1:T(4,128)} %get-tuple-element.40, ...), dimensions={0} | concatenate | bytes 3145728 | tf_op jit(solution)/shard_map/concatenate | solution.py:82
  485.4 11.4 %concatenate.64 = f32[24,8,16,128]{3,0,2,1:T(8,128)S(1)} concatenate(f32[3,8,16,128]{3,0,2,1:T(4,128)S(1)} %copy.26, f32[3,8,16,128]{3,0,2,1:T(4,128)} %get-tuple-element.20, f32[3,8,16,128]{3,0,2,1:T(4,128)} %get-tuple-element.52, f32[3,8,16,128]{3,0,2,1:T(4,128)} %get-tuple-element.19, f32[3,8,16,128]{3,0,2,1:T(4,128)} %pad_maximum_fusion.8, ...), dimensions={0} | concatenate | bytes 3145728 | tf_op jit(solution)/shard_map/concatenate | solution.py:82
  496.8 1.6 multiply_reduce_fusion
  498.4 113.7 %scatter_custom_fusion = f32[128]{0:T(128)S(1)} fusion(s32[16384]{0:T(1024)} %bitcast.38, f32[16384]{0:T(1024)S(1)} %bitcast.41, f32[]{:T(128)} %constant.21.clone.1), kind=kCustom, calls=%fused_computation.79 | custom fusion | flops 16384 | bytes 1024 | tf_op jit(solution)/shard_map/scatter-add | solution.py:160
  612.0 40.7 %all-reduce.1 = f32[128]{0:T(128)S(1)} all-reduce(f32[128]{0:T(128)S(1)} %scatter_custom_fusion), channel_id=2, replica_groups=mesh['gx'=2,'gy'=4,'gz'=4] {'gx','gy','gz'}, use_global_device_ids=true, to_apply=%region_10.11.clone | all-reduce | flops 128 | bytes 1024
  652.7 0.6 dynamic-slice
  (57 shorter events, 0.4 us)
Async XLA Ops:
  0.6 47.7 %copy-start = (s32[128]{0:T(128)S(1)}, s32[128]{0:T(128)}, u32[]{:S(2)}) copy-start(s32[128]{0:T(128)} %param.11) | copy-start | bytes 1540
  1.5 247.6 %collective-permute-start = (f32[3,2,16,128]{3,0,2,1:T(4,128)S(1)}, f32[3,2,16,128]{3,0,2,1:T(4,128)S(1)}, u32[]{:S(2)}, u32[]{:S(2)}) collective-permute-start(f32[3,2,16,128]{3,0,2,1:T(4,128)S(1)} %copy.37), channel_id=1, source_target_pairs={{0,16},{1,17},{2,18},{3,19},{4,20},{5,21},{6,22},{7,23},{8,24},{9,... | collective-permute-start | bytes 147464 | tf_op jit(solution)/shard_map/ppermute | solution.py:20
  3.9 245.4 %collective-permute-start.1 = (f32[3,2,16,128]{3,0,2,1:T(4,128)S(1)}, f32[3,2,16,128]{3,0,2,1:T(4,128)S(1)}, u32[]{:S(2)}, u32[]{:S(2)}) collective-permute-start(f32[3,2,16,128]{3,0,2,1:T(4,128)S(1)} %copy.38), channel_id=1, source_target_pairs={{16,0},{17,1},{18,2},{19,3},{20,4},{21,5},{22,6},{23,7},{24,8},{25... | collective-permute-start | bytes 147464 | tf_op jit(solution)/shard_map/ppermute | solution.py:21
  48.3 97.2 %copy-start.15 = (s32[8,16,128]{2,1,0:T(8,128)S(1)}, s32[8,16,128]{2,1,0:T(8,128)}, u32[]{:S(2)}) copy-start(s32[8,16,128]{2,1,0:T(8,128)} %param.10) | copy-start | bytes 196612
  48.4 97.3 %copy-start.17 = (f32[3,8,16,128]{3,2,1,0:T(8,128)S(1)}, f32[3,8,16,128]{3,2,1,0:T(8,128)}, u32[]{:S(2)}) copy-start(f32[3,8,16,128]{3,2,1,0:T(8,128)} %param.7) | copy-start | bytes 589828
  145.6 97.4 %copy-start.16 = (s32[8,16,128]{2,1,0:T(8,128)}, s32[8,16,128]{2,1,0:T(8,128)S(1)}, u32[]{:S(2)}) copy-start(s32[8,16,128]{2,1,0:T(8,128)S(1)} %get-tuple-element.16) | copy-start | bytes 196612
  145.8 97.3 %copy-start.13 = (s32[8,16,128]{2,1,0:T(8,128)S(1)}, s32[8,16,128]{2,1,0:T(8,128)}, u32[]{:S(2)}) copy-start(s32[8,16,128]{2,1,0:T(8,128)} %param.9) | copy-start | bytes 196612
  145.8 102.6 %copy-start.2 = (f32[3,8,16,128]{3,2,1,0:T(8,128)S(1)}, f32[3,8,16,128]{3,2,1,0:T(8,128)}, u32[]{:S(2)}) copy-start(f32[3,8,16,128]{3,2,1,0:T(8,128)} %param.8) | copy-start | bytes 589828
  243.2 12.3 %collective-permute-start.7 = (f32[4,2,16,128]{3,0,2,1:T(4,128)S(1)}, f32[4,2,16,128]{3,0,2,1:T(4,128)S(1)}, u32[]{:S(2)}, u32[]{:S(2)}) collective-permute-start(f32[4,2,16,128]{3,0,2,1:T(4,128)S(1)} %get-tuple-element.56), channel_id=1, source_target_pairs={{16,0},{17,1},{18,2},{19,3},{20,4},{21,5},{22,6},{23,7},{24,8},{25... | collective-permute-start | bytes 196616 | tf_op jit(solution)/shard_map/ppermute | solution.py:21
  244.5 11.0 %collective-permute-start.6 = (f32[4,2,16,128]{3,0,2,1:T(4,128)S(1)}, f32[4,2,16,128]{3,0,2,1:T(4,128)S(1)}, u32[]{:S(2)}, u32[]{:S(2)}) collective-permute-start(f32[4,2,16,128]{3,0,2,1:T(4,128)S(1)} %get-tuple-element.55), channel_id=1, source_target_pairs={{0,16},{1,17},{2,18},{3,19},{4,20},{5,21},{6,22},{7,23},{8,24},{9,... | collective-permute-start | bytes 196616 | tf_op jit(solution)/shard_map/ppermute | solution.py:20
  249.4 13.6 %collective-permute-start.3 = (f32[3,12,2,128]{3,0,2,1:T(4,128)S(1)}, f32[3,12,2,128]{3,0,2,1:T(4,128)S(1)}, u32[]{:S(2)}, u32[]{:S(2)}) collective-permute-start(f32[3,12,2,128]{3,0,2,1:T(4,128)S(1)} %get-tuple-element.54), channel_id=1, source_target_pairs={{4,0},{8,4},{12,8},{5,1},{9,5},{13,9},{6,2},{10,6},{14,10},{7,3},{... | collective-permute-start | bytes 110600 | tf_op jit(solution)/shard_map/ppermute | solution.py:21
  250.7 12.3 %collective-permute-start.2 = (f32[3,12,2,128]{3,0,2,1:T(4,128)S(1)}, f32[3,12,2,128]{3,0,2,1:T(4,128)S(1)}, u32[]{:S(2)}, u32[]{:S(2)}) collective-permute-start(f32[3,12,2,128]{3,0,2,1:T(4,128)S(1)} %get-tuple-element.53), channel_id=1, source_target_pairs={{0,4},{4,8},{8,12},{1,5},{5,9},{9,13},{2,6},{6,10},{10,14},{3,7},{... | collective-permute-start | bytes 110600 | tf_op jit(solution)/shard_map/ppermute | solution.py:20
  256.2 88.1 %collective-permute-start.9 = (f32[4,12,2,128]{3,0,2,1:T(4,128)}, f32[4,12,2,128]{3,0,2,1:T(4,128)S(1)}, u32[]{:S(2)}, u32[]{:S(2)}) collective-permute-start(f32[4,12,2,128]{3,0,2,1:T(4,128)} %get-tuple-element.50), channel_id=1, source_target_pairs={{4,0},{8,4},{12,8},{5,1},{9,5},{13,9},{6,2},{10,6},{14,10},{7,3},{... | collective-permute-start | bytes 147464 | tf_op jit(solution)/shard_map/ppermute | solution.py:21
  257.5 86.8 %collective-permute-start.8 = (f32[4,12,2,128]{3,0,2,1:T(4,128)}, f32[4,12,2,128]{3,0,2,1:T(4,128)S(1)}, u32[]{:S(2)}, u32[]{:S(2)}) collective-permute-start(f32[4,12,2,128]{3,0,2,1:T(4,128)} %get-tuple-element.49), channel_id=1, source_target_pairs={{0,4},{4,8},{8,12},{1,5},{5,9},{9,13},{2,6},{6,10},{10,14},{3,7},{... | collective-permute-start | bytes 147464 | tf_op jit(solution)/shard_map/ppermute | solution.py:20
  262.9 15.2 %copy-start.9 = (f32[3,12,2,128]{3,0,2,1:T(4,128)}, f32[3,12,2,128]{3,0,2,1:T(4,128)S(1)}, u32[]{:S(2)}) copy-start(f32[3,12,2,128]{3,0,2,1:T(4,128)S(1)} %collective-permute-done.3) | copy-start | bytes 110596
  263.0 15.2 %copy-start.11 = (f32[3,12,2,128]{3,0,2,1:T(4,128)}, f32[3,12,2,128]{3,0,2,1:T(4,128)S(1)}, u32[]{:S(2)}) copy-start(f32[3,12,2,128]{3,0,2,1:T(4,128)S(1)} %collective-permute-done.2) | copy-start | bytes 110596
  263.4 13.6 %collective-permute-start.5 = (f32[3,12,20,2]{3,0,2,1:T(4,128)S(1)}, f32[3,12,20,2]{3,0,2,1:T(4,128)S(1)}, u32[]{:S(2)}, u32[]{:S(2)}) collective-permute-start(f32[3,12,20,2]{3,0,2,1:T(4,128)S(1)} %get-tuple-element.46), channel_id=1, source_target_pairs={{1,0},{2,1},{3,2},{5,4},{6,5},{7,6},{9,8},{10,9},{11,10},{13,12},{... | collective-permute-start | bytes 17288 | tf_op jit(solution)/shard_map/ppermute | solution.py:21
  264.7 13.4 %collective-permute-start.4 = (f32[3,12,20,2]{3,0,2,1:T(4,128)S(1)}, f32[3,12,20,2]{3,0,2,1:T(4,128)S(1)}, u32[]{:S(2)}, u32[]{:S(2)}) collective-permute-start(f32[3,12,20,2]{3,0,2,1:T(4,128)S(1)} %get-tuple-element.45), channel_id=1, source_target_pairs={{0,1},{1,2},{2,3},{4,5},{5,6},{6,7},{8,9},{9,10},{10,11},{12,13},{... | collective-permute-start | bytes 17288 | tf_op jit(solution)/shard_map/ppermute | solution.py:20
  277.0 6.7 %copy-start.4 = (f32[3,12,20,2]{3,0,2,1:T(4,128)}, f32[3,12,20,2]{3,0,2,1:T(4,128)S(1)}, u32[]{:S(2)}) copy-start(f32[3,12,20,2]{3,0,2,1:T(4,128)S(1)} %collective-permute-done.5) | copy-start | bytes 17284
  344.5 18.2 %copy-start.1 = (f32[24,11,19,131]{3,0,2,1:T(8,128)S(1)}, f32[24,11,19,131]{3,0,2,1:T(8,128)}, u32[]{:S(2)}) copy-start(f32[24,11,19,131]{3,0,2,1:T(8,128)} %concatenate.52) | copy-start | bytes 7885156
  344.5 18.2 %copy-start.18 = (f32[24,24,1,1]{1,0,3,2:T(8,128)S(1)}, f32[24,24,1,1]{1,0,3,2:T(8,128)}, u32[]{:S(2)}) copy-start(f32[24,24,1,1]{1,0,3,2:T(8,128)} %constant.81) | copy-start | bytes 6916
  344.8 12.6 %collective-permute-start.10 = (f32[4,12,20,2]{3,0,2,1:T(4,128)S(1)}, f32[4,12,20,2]{3,0,2,1:T(4,128)S(1)}, u32[]{:S(2)}, u32[]{:S(2)}) collective-permute-start(f32[4,12,20,2]{3,0,2,1:T(4,128)S(1)} %get-tuple-element.47), channel_id=1, source_target_pairs={{0,1},{1,2},{2,3},{4,5},{5,6},{6,7},{8,9},{9,10},{10,11},{12,13},{... | collective-permute-start | bytes 23048 | tf_op jit(solution)/shard_map/ppermute | solution.py:20
  349.5 12.1 %collective-permute-start.11 = (f32[4,12,20,2]{3,0,2,1:T(4,128)S(1)}, f32[4,12,20,2]{3,0,2,1:T(4,128)S(1)}, u32[]{:S(2)}, u32[]{:S(2)}) collective-permute-start(f32[4,12,20,2]{3,0,2,1:T(4,128)S(1)} %get-tuple-element.48), channel_id=1, source_target_pairs={{1,0},{2,1},{3,2},{5,4},{6,5},{7,6},{9,8},{10,9},{11,10},{13,12},{... | collective-permute-start | bytes 23048 | tf_op jit(solution)/shard_map/ppermute | solution.py:21
  361.6 1.0 copy-start.6
  362.7 5.0 copy-start.8
  415.4 5.7 copy-start.3
  415.4 54.8 %copy-start.5 = (f32[3,12,20,2]{3,0,2,1:T(4,128)S(1)}, f32[3,12,20,2]{3,0,2,1:T(4,128)}, u32[]{:S(2)}) copy-start(f32[3,12,20,2]{3,0,2,1:T(4,128)} %copy-done.4) | copy-start | bytes 17284
  415.4 54.8 %copy-start.10 = (f32[3,12,2,128]{3,0,2,1:T(4,128)S(1)}, f32[3,12,2,128]{3,0,2,1:T(4,128)}, u32[]{:S(2)}) copy-start(f32[3,12,2,128]{3,0,2,1:T(4,128)} %copy-done.9) | copy-start | bytes 110596
  415.4 54.8 %copy-start.12 = (f32[3,12,2,128]{3,0,2,1:T(4,128)S(1)}, f32[3,12,2,128]{3,0,2,1:T(4,128)}, u32[]{:S(2)}) copy-start(f32[3,12,2,128]{3,0,2,1:T(4,128)} %copy-done.11) | copy-start | bytes 110596
  422.6 50.3 %copy-start.7 = (f32[4,12,20,2]{3,0,2,1:T(4,128)S(1)}, f32[4,12,20,2]{3,0,2,1:T(4,128)}, u32[]{:S(2)}) copy-start(f32[4,12,20,2]{3,0,2,1:T(4,128)} %copy-done.6) | copy-start | bytes 23044
  485.4 13.0 %copy-start.14 = (s32[8,16,128]{2,1,0:T(8,128)S(1)}, s32[8,16,128]{2,1,0:T(8,128)}, u32[]{:S(2)}) copy-start(s32[8,16,128]{2,1,0:T(8,128)} %param.9) | copy-start | bytes 196612
where the time goes:
time: 659 us; the launch traced here: 653 us
  local copies, waits for them, and re-layouts  336 us (51%)
  other arithmetic  125 us (19%)
  blocking collectives  122 us (19%)
  starting transfers between devices  32.8 us (5%)
  waiting for transfers between devices  16.7 us (3%)
  matrix products  12.3 us (2%)
  between operations  8.81 us (1%)
    concatenate x4, local copies, waits for them, and re-layouts, corner_stack(): return jnp.concatenate(pieces, axis=0)  125 us
    scatter-add x1, other arithmetic, on_device(): jax.ops.segment_sum(terms.ravel(), slot_map.ravel(), num_segments=zone_co...  114 us
    gather x1, local copies, waits for them, and re-layouts, on_device(): slot_map = jnp.take(zone_slot, elem_zone)  97.2 us
    gather x1, local copies, waits for them, and re-layouts, on_device(): moduli = jnp.take(all_moduli, slot_map) * bone_float  97.2 us
    unnamed x2, blocking collectives  82 us
    psum x1, blocking collectives, on_device(): lax.psum((jnp.sum(adjoint_load * adjoint_load), jnp.sum(adjoint_load * kr...  40 us
    ppermute x6, starting transfers between devices, with_halo(): before = lax.ppermute(last, axis, up)  24.9 us
  transfers between devices with their start and end apart: 12, of which 4 were waited for; matrix products, arithmetic and copies ran while one was open for 41% of the time, Pallas kernels for 0%

commit v1 on v0

v1 whole, which is shorter than its diff:
```python
import functools
import jax
import jax.numpy as jnp
from jax import lax
from jax.experimental import pallas as pl
from jax.experimental.pallas import tpu as pltpu
from jax.sharding import PartitionSpec as P

ZS = 16
SPRING = 0.1
MESH = pl.DeviceIdType.MESH
LAME = 0.3 / (1.3 * 0.4)
SHEAR = 0.5 / 1.3
F32 = jnp.float32
LOW = 5


def element_forces(m):
    c = 1.0 / 16.0
    lam, mu = c * LAME, c * SHEAR
    lam3, mu3 = lam / 3.0, mu / 3.0
    u, v, w = m
    f = [[[[None, None], [None, None]], [[None, None], [None, None]]] for _ in range(3)]
    div = lam * (u[1][0][0] + v[0][1][0] + w[0][0][1])
    f[0][1][0][0] = div + (2 * mu) * u[1][0][0]
    f[1][0][1][0] = div + (2 * mu) * v[0][1][0]
    f[2][0][0][1] = div + (2 * mu) * w[0][0][1]
    f[0][0][1][0] = f[1][1][0][0] = mu * (u[0][1][0] + v[1][0][0])
    f[1][0][0][1] = f[2][0][1][0] = mu * (v[0][0][1] + w[0][1][0])
    f[0][0][0][1] = f[2][1][0][0] = mu * (u[0][0][1] + w[1][0][0])
    t = lam3 * (u[1][1][0] + w[0][1][1])
    f[0][1][1][0] = t + mu * u[1][1][0]
    f[2][0][1][1] = t + mu * w[0][1][1]
    t = lam3 * (u[1][0][1] + v[0][1][1])
    f[0][1][0][1] = t + mu * u[1][0][1]
    f[1][0][1][1] = t + mu * v[0][1][1]
    t = lam3 * (v[1][1][0] + w[1][0][1])
    f[1][1][1][0] = t + mu * v[1][1][0]
    f[2][1][0][1] = t + mu * w[1][0][1]
    t = u[0][1][1] + v[1][0][1] + w[1][1][0]
    f[0][0][1][1] = mu3 * (t + u[0][1][1])
    f[1][1][0][1] = mu3 * (t + v[1][0][1])
    f[2][1][1][0] = mu3 * (t + w[1][1][0])
    for k in range(3):
        f[k][1][1][1] = ((lam + 4 * mu) / 9.0) * m[k][1][1][1]
    return f


def modes_of(load, x):
    out = []
    for k in range(3):
        here = [[load(4 * k + 2 * b + c, x) for c in range(2)] for b in range(2)]
        there = [[load(4 * k + 2 * b + c, x + 1) for c in range(2)] for b in range(2)]
        out.append([
            [[None if b + c == 0 else there[b][c] + here[b][c] for c in range(2)] for b in range(2)],
            [[there[b][c] - here[b][c] for c in range(2)] for b in range(2)],
        ])
    return out


ALL = [(k, a, b, c) for k in range(3) for a in range(2) for b in range(2) for c in range(2) if a + b + c]


def dot_modes(f, g):
    total = None
    for k, a, b, c in ALL:
        t = f[k][a][b][c] * g[k][a][b][c]
        total = t if total is None else total + t
    return total


def kernel(sizes, disp, load, mask, zone, slot_ref, mod_ref, adj_ref, grad_ref,
           E, BM, DM, NB, Q, QM, TB, G, MS, R, ZPL, ZPH, ZL, ZH, YPL, YPH, YL, YH,
           ag_send, ag_recv, rs_send, rs_recv, hs, hr):
    nx, ny, nz = sizes
    n = nx * ny * nz
    cx, cy, cz = mask.shape
    wy, wz = cy + 8, 2 * cz
    per = mod_ref.shape[0]
    rows = slot_ref.shape[0]
    ix, iy, iz = lax.axis_index("gx"), lax.axis_index("gy"), lax.axis_index("gz")
    me = (ix * ny + iy) * nz + iz

    def place(t):
        return (t // (ny * nz), (t // nz) % ny, t % nz)

    lane1 = lax.broadcasted_iota(jnp.int32, (1, 128), 1)
    row = jnp.zeros((1, 128), F32)
    for j in range(per):
        row = jnp.where(lane1 == (me * per) % 128 + j, mod_ref[j], row)
    G[me] = row

    def send_mod(o, carry):
        t = (me + o) % n
        pltpu.make_async_remote_copy(
            src_ref=G.at[me], dst_ref=G.at[me], send_sem=ag_send, recv_sem=ag_recv,
            device_id=place(t), device_id_type=MESH).start()
        return carry
    lax.fori_loop(1, n, send_mod, 0)

    def exchange(axis, spot, count, low_src, high_dst, high_src, low_dst, s):
        down = pltpu.make_async_remote_copy(
            src_ref=low_src, dst_ref=high_dst, send_sem=hs.at[s], recv_sem=hr.at[s],
            device_id={axis: jnp.maximum(spot - 1, 0)}, device_id_type=MESH)
        up = pltpu.make_async_remote_copy(
            src_ref=high_src, dst_ref=low_dst, send_sem=hs.at[s + 1], recv_sem=hr.at[s + 1],
            device_id={axis: jnp.minimum(spot + 1, count - 1)}, device_id_type=MESH)

        @pl.when(spot > 0)
        def _():
            down.start()

        @pl.when(spot < count - 1)
        def _():
            up.start()

        @pl.when(spot == 0)
        def _():
            low_dst[...] = jnp.zeros(low_dst.shape, F32)

        @pl.when(spot == count - 1)
        def _():
            high_dst[...] = jnp.zeros(high_dst.shape, F32)

        @pl.when(spot > 0)
        def _():
            down.wait_send()
            up.wait_recv()

        @pl.when(spot < count - 1)
        def _():
            up.wait_send()
            down.wait_recv()

    lane = lax.broadcasted_iota(jnp.int32, (cy, 128), 1)

    def fill(x, carry):
        low, high = carry
        for f in range(8):
            if f < 3:
                value = load[f, x]
            elif f == 3:
                value = mask[x].astype(F32)
            elif f == 4:
                value = zone[x].astype(F32)
            else:
                value = disp[f - 5, x]
            E[f, x + 1, 0:cy, 0:cz] = value
            low = jnp.where(lane == f * 8 + x, pltpu.roll(value, f * 8 + x, 1), low)
            if f < 3:
                low = jnp.where(lane == (8 + f) * 8 + x, pltpu.roll(value, (8 + f) * 8 + x - 1, 1), low)
            if f < LOW:
                high = jnp.where(lane == f * 8 + x, pltpu.roll(value, f * 8 + x + 1, 1), high)
        return low, high
    zero = jnp.zeros((cy, 128), F32)
    low, high = lax.fori_loop(0, cx, fill, (zero, zero))
    ZPL[...] = low
    ZPH[...] = high
    exchange("gz", iz, nz, ZPL, ZH, ZPH, ZL, 0)

    def open_z(x, carry):
        above, below = ZH[...], ZL[...]
        for f in range(8):
            tile = jnp.where(lane == 0, pltpu.roll(above, 128 - f * 8 - x, 1), 0.0)
            if f < 3:
                tile = jnp.where(lane == 1, pltpu.roll(above, 128 + 1 - (8 + f) * 8 - x, 1), tile)
            if f < LOW:
                tile = jnp.where(lane == 127, pltpu.roll(below, 127 - f * 8 - x, 1), tile)
            E[f, x + 1, 0:cy, cz:wz] = tile
        return carry
    lax.fori_loop(0, cx, open_z, 0)

    for f in range(8):
        YPL[f] = E[f, 1:cx + 1, 0, :]
        if f < 3:
            YPL[8 + f] = E[f, 1:cx + 1, 1, :]
        if f < LOW:
            YPH[f] = E[f, 1:cx + 1, cy - 1, :]
    exchange("gy", iy, ny, YPL, YH, YPH, YL, 2)
    line = lax.broadcasted_iota(jnp.int32, (8, wz), 0)
    for f in range(8):
        above = YH[f]
        second = YH[8 + f] if f < 3 else None
        below = YL[f] if f < LOW else None
        for x in range(cx):
            tile = jnp.where(line == 0, above[x:x + 1], 0.0)
            if f < 3:
                tile = jnp.where(line == 1, second[x:x + 1], tile)
            if f < LOW:
                tile = jnp.where(line == 7, below[x:x + 1], tile)
            E[f, x + 1, cy:wy, :] = tile
    exchange("gx", ix, nx, E.at[:, pl.ds(1, 2)], E.at[:, pl.ds(cx + 1, 2)],
             E.at[pl.ds(0, LOW), pl.ds(cx, 1)], E.at[pl.ds(0, LOW), pl.ds(0, 1)], 4)

    whole = G.at[pl.ds(0, n - 1)]
    pltpu.make_async_copy(whole, whole, ag_recv).wait()
    pltpu.make_async_copy(whole, whole, ag_send).wait()
    group = n // rows
    by_slot = [jnp.sum(G[g * group:(g + 1) * group, 0, :], axis=0, keepdims=True) for g in range(rows)]

    def look_up(tables, index):
        tables = [jnp.broadcast_to(t, (8, 128)) for t in tables]
        low_bits, which = index % 128, index // 128
        out = None
        for g, t in enumerate(tables):
            got = jnp.take_along_axis(t, low_bits, axis=1, mode="promise_in_bounds")
            out = got if out is None else jnp.where(which == g, got, out)
        return out
    by_zone = []
    for g in range(rows):
        index = jnp.broadcast_to(slot_ref[g:g + 1, :], (8, 128))
        by_zone.append(look_up(by_slot, index)[0:1])

    def yz_modes(v, put, x, k):
        after = pltpu.roll(v, wz - 1, 1)
        for c, t in enumerate((v + after, after - v)):
            above = pltpu.roll(t, wy - 1, 0)
            put(4 * k + c, x, t + above)
            put(4 * k + 2 + c, x, above - t)

    def put_b(i, x, v):
        BM[i, x] = v

    def put_d(i, x, v):
        DM[i, x] = v[0:cy, 0:cz]

    def put_q(i, x, v):
        QM[i, x] = v[0:cy, 0:cz]

    def b_modes(x, carry):
        for k in range(3):
            yz_modes(E[k, x], put_b, x, k)
        return carry
    lax.fori_loop(0, cx + 3, b_modes, 0)

    def d_modes(x, carry):
        for k in range(3):
            yz_modes(E[5 + k, x + 1], put_d, x, k)
        return carry
    lax.fori_loop(0, cx + 1, d_modes, 0)

    def first(x, carry):
        where = E[4, x].astype(jnp.int32)
        parts = []
        for y in range(0, wy, 8):
            parts.append(jnp.concatenate(
                [look_up(by_zone, where[y:y + 8, z:z + 128]) for z in range(0, wz, 128)], axis=1))
        stiff = jnp.where(E[3, x] > 0.5, jnp.concatenate(parts, axis=0), 0.0)
        TB[1, x] = stiff[0:cy, 0:cz]
        f = element_forces(modes_of(lambda i, p: BM[i, p], x))

        @pl.when(jnp.logical_and(x > 0, x <= cx))
        def _():
            inner = [[[[None if t is None else t[0:cy, 0:cz] for t in b] for b in a] for a in k] for k in f]
            TB[0, x] = dot_modes(inner, modes_of(lambda i, p: DM[i, p], x - 1))
        for k in range(3):
            for b in range(2):
                for c in range(2):
                    i = 4 * k + 2 * b + c
                    delta = f[k][1][b][c] * stiff
                    if b + c:
                        total = f[k][0][b][c] * stiff
                        now, later = total - delta, total + delta
                    else:
                        now, later = -delta, delta
                    NB[i, x] = NB[i, x] + now
                    NB[i, x + 1] = later
        return carry
    for i in range(12):
        NB[i, 0] = jnp.zeros((wy, wz), F32)
    lax.fori_loop(0, cx + 2, first, 0)

    at_y = lax.broadcasted_iota(jnp.int32, (wy, wz), 0)
    at_z = lax.broadcasted_iota(jnp.int32, (wy, wz), 1)
    last_x, last_y, last_z = ix == nx - 1, iy == ny - 1, iz == nz - 1
    keep_y = jnp.where(last_y, cy, wy)
    keep_z = jnp.where(last_z, cz, wz)
    inside = jnp.logical_and(at_y < keep_y, at_z < keep_z)

    def nodes(x, carry):
        bq, qq, bb = carry
        keep_x = jnp.where(last_x, cx, cx + 1)
        valid = jnp.logical_and(inside, jnp.broadcast_to(x, (wy, wz)) < keep_x)
        own = jnp.where(x < cx, 1.0, 0.0).astype(F32)
        for k in range(3):
            side = []
            for c in range(2):
                s, d = NB[4 * k + c, x + 1], NB[4 * k + 2 + c, x + 1]
                side.append((s - d) + pltpu.roll(s + d, 1, 0))
            q = (side[0] - side[1]) + pltpu.roll(side[0] + side[1], 1, 1)
            q = jnp.where(valid, q, 0.0)
            mine = q[0:cy, 0:cz]
            Q[k, x] = mine
            v = E[k, x + 1, 0:cy, 0:cz]
            bq = bq + own * (v * mine)
            qq = qq + own * (mine * mine)
            bb = bb + own * (v * v)
            yz_modes(q, put_q, x, k)
        return bq, qq, bb
    bq, qq, bb = lax.fori_loop(0, cx + 1, nodes, (zero, zero, zero))

    scale = -(ZS ** -1.5)
    first_zone = zone[0]

    def second(x, carry):
        energy, a1, a2, b1, b2 = carry
        m = modes_of(lambda i, p: QM[i, p], x)
        f = element_forces(m)
        energy = energy + TB[1, x + 1] * dot_modes(f, m)
        bone = scale * mask[x].astype(F32)
        t2 = bone * dot_modes(f, modes_of(lambda i, p: DM[i, p], x))
        t1 = bone * TB[0, x + 1]
        same = zone[x] == first_zone
        a1 = a1 + jnp.where(same, t1, 0.0)
        a2 = a2 + jnp.where(same, t2, 0.0)
        b1 = b1 + jnp.where(same, 0.0, t1)
        b2 = b2 + jnp.where(same, 0.0, t2)
        return energy, a1, a2, b1, b2
    energy, a1, a2, b1, b2 = lax.fori_loop(0, cx, second, (zero,) * 5)

    owner = lax.broadcasted_iota(jnp.int32, (n, 128), 0)
    sub = lax.broadcasted_iota(jnp.int32, (16, 128), 0)
    slots = [slot_ref[g:g + 1, :] for g in range(rows)]
    out = jnp.zeros((n, 16), F32)
    for zones, t1, t2 in ((first_zone, a1, a2), (zone[cx - 1], b1, b2)):
        same = zones == zones[0:1]
        for at, cond in ((0, same), (cy - 1, jnp.logical_not(same))):
            v1 = jnp.sum(jnp.where(cond, t1, 0.0), axis=0, keepdims=True)
            v2 = jnp.sum(jnp.where(cond, t2, 0.0), axis=0, keepdims=True)
            k = look_up(slots, jnp.broadcast_to(zones[at:at + 1], (8, 128)))[0:1]
            own_by, part = k // per, k % per
            w = jnp.where(owner == own_by, 1.0, 0.0).astype(F32)
            v = jnp.where(sub == part, v1, jnp.where(sub == part + per, v2, 0.0))
            out = out + lax.dot_general(w, v, (((1,), (1,)), ((), ())),
                                        precision=lax.Precision.HIGHEST, preferred_element_type=F32)
    lane16 = lax.broadcasted_iota(jnp.int32, (n, 16), 1)
    for j, value in enumerate((bb, bq, qq, energy)):
        value = jnp.sum(jnp.sum(value, axis=0, keepdims=True), axis=1, keepdims=True)
        out = jnp.where(lane16 == 2 * per + j, value, out)
    MS[...] = jnp.zeros_like(MS)
    MS[:, 0, 0:16] = out

    def send_sum(o, carry):
        t = (me + o) % n
        pltpu.make_async_remote_copy(
            src_ref=MS.at[t], dst_ref=R.at[n - 1 - o], send_sem=rs_send, recv_sem=rs_recv,
            device_id=place(t), device_id_type=MESH).start()
        return carry
    lax.fori_loop(1, n, send_sum, 0)
    pltpu.make_async_copy(R, R, rs_recv).wait()
    pltpu.make_async_copy(R, R, rs_send).wait()
    row = jnp.sum(R[:, 0, :], axis=0, keepdims=True) + MS[me]

    def pick(j):
        return jnp.sum(jnp.where(lane1 == 2 * per + j, row, 0.0), axis=1, keepdims=True)
    bb, bq, qq, qkq = pick(0), pick(1), pick(2), pick(3)
    gram = bb * qq - bq * bq
    top = SPRING * gram + (bb * qkq - bq * qq)
    det = SPRING * top + (bq * qkq - qq * qq)
    plane = det != 0.0
    c1 = jnp.where(plane, top / det, bb / (SPRING * bb + bq))
    c2 = jnp.where(plane, -gram / det, 0.0)
    both = c1 * row + c2 * pltpu.roll(row, 128 - per, 1)
    grad_ref[...] = both[:, 0:per]

    def finish(x, carry):
        for k in range(3):
            adj_ref[k, x] = c1 * load[k, x] + c2 * Q[k, x]
        return carry
    lax.fori_loop(0, cx, finish, 0)


def solution(mesh):
    sizes = (mesh.shape["gx"], mesh.shape["gy"], mesh.shape["gz"])
    n = sizes[0] * sizes[1] * sizes[2]

    def on_device(displacement, adjoint_load, bone_mask, elem_zone, zone_slot, zone_modulus):
        cx, cy, cz = bone_mask.shape
        per = zone_modulus.shape[0]
        wy, wz = cy + 8, 2 * cz
        vm = pl.BlockSpec(memory_space=pltpu.VMEM)
        scratch = [
            (8, cx + 3, wy, wz), (12, cx + 3, wy, wz), (12, cx + 1, cy, cz), (12, cx + 3, wy, wz),
            (3, cx + 1, cy, cz), (12, cx + 1, cy, cz), (2, cx + 2, cy, cz),
            (n, 1, 128), (n, 1, 128), (n - 1, 1, 128),
            (cy, 128), (cy, 128), (cy, 128), (cy, 128),
            (11, cx, wz), (LOW, cx, wz), (LOW, cx, wz), (11, cx, wz),
        ]
        adjoint, gradient = pl.pallas_call(
            functools.partial(kernel, sizes),
            out_shape=(jax.ShapeDtypeStruct(adjoint_load.shape, F32), jax.ShapeDtypeStruct((1, per), F32)),
            in_specs=[vm] * 5 + [pl.BlockSpec(memory_space=pltpu.SMEM)],
            out_specs=(vm, vm),
            scratch_shapes=[pltpu.VMEM(s, F32) for s in scratch]
            + [pltpu.SemaphoreType.DMA] * 4 + [pltpu.SemaphoreType.DMA((6,))] * 2,
            compiler_params=pltpu.CompilerParams(has_side_effects=True, vmem_limit_bytes=40 * 2**20),
            cost_estimate=pl.CostEstimate(flops=10**7, bytes_accessed=10**6, transcendentals=0),
        )(displacement, adjoint_load, bone_mask, elem_zone, zone_slot.reshape(-1, 128), zone_modulus)
        return adjoint, gradient.reshape(per)

    whole = P(None, "gx", "gy", "gz")
    brick = P("gx", "gy", "gz")
    owned = P(("gx", "gy", "gz"))
    return jax.shard_map(on_device, mesh=mesh, in_specs=(whole, whole, brick, brick, P(), owned),
                         out_specs=(whole, owned), check_vma=False)
```

time: 659 us -> 38.4 us (0.06)
  local copies, waits for them, and re-layouts: 336 us -> 5.38 us
  other arithmetic: 125 us -> 0 us
  blocking collectives: 122 us -> 0 us
  starting transfers between devices: 32.8 us -> 0 us
  Pallas kernels: 0 us -> 32.1 us
  waiting for transfers between devices: 16.7 us -> 0 us
  matrix products: 12.3 us -> 0 us
  between operations: 8.81 us -> 0.66 us
    gather x2 -> x0, local copies, waits for them, and re-layouts: 194 us -> none  [the longest x1 97.2 us: on_device(): slot_map = jnp.take(zone_slot, elem_zone)]
    concatenate x5 -> x0, local copies, waits for them, and re-layouts: 125 us -> none  [the longest x4 125 us: corner_stack(): return jnp.concatenate(pieces, axis=0)]
    scatter-add x1 -> x0, other arithmetic: 114 us -> none  [on_device(): jax.ops.segment_sum(terms.ravel(), slot_map.ravel(), num_segments=zone_co...]
    unnamed x2 -> x0, blocking collectives: 82 us -> none
    psum x1 -> x0, blocking collectives: 40 us -> none  [on_device(): lax.psum((jnp.sum(adjoint_load * adjoint_load), jnp.sum(adjoint_load * kr...]
    ppermute x12 -> x0, starting transfers between devices: 32.8 us -> none  [the longest x6 24.9 us: with_halo(): before = lax.ppermute(last, axis, up)]
    pallas_call x0 -> x1, Pallas kernels: none -> 32.1 us  [on_device(): pl.pallas_call(functools.partial(kernel, sizes), out_shape=(jax.ShapeDtyp...]
    ppermute x12 -> x0, waiting for transfers between devices: 16.7 us -> none  [the longest x6 10.2 us: with_halo(): after = lax.ppermute(leading, axis, down)]
  transfers between devices with their start and end apart: 12 -> 0, of which waited for: 4 -> 0; matrix products, arithmetic and copies ran while one was open for 41% -> 0% of each run, Pallas kernels for 0% -> 0%
where the time goes in v1:
time: 38.4 us; the launch traced here: 38.2 us
  Pallas kernels  32.1 us (84%)
  local copies, waits for them, and re-layouts  5.38 us (14%)
  between operations  0.66 us (2%)
    pallas_call x1, Pallas kernels, on_device(): pl.pallas_call(functools.partial(kernel, sizes), out_shape=(jax.ShapeDtyp...  32.1 us
    unnamed x14, local copies, waits for them, and re-layouts  5.38 us

profile of v1, /device:TPU:0, one launch (start us, length us, event | category | flops | bytes accessed | tf_op | source)
XLA Modules:
  0.0 38.2 jit_solution(9682429354160805430)
XLA Ops:
  0.6 0.0 copy-start.5
  0.6 0.0 copy-start.4
  0.7 0.6 %copy-done.5 = f32[4]{0:T(128)S(1)} copy-done((f32[4]{0:T(128)S(1)}, f32[4]{0:T(128)}, u32[]{:S(2)}) %copy-start.5) | copy-done | bytes 40
  1.3 0.0 copy-done.4
  1.3 0.0 copy-start
  1.3 0.9 %copy-done = f32[3,8,16,128]{3,2,1,0:T(8,128)S(1)} copy-done((f32[3,8,16,128]{3,2,1,0:T(8,128)S(1)}, f32[3,8,16,128]{3,2,1,0:T(8,128)}, u32[]{:S(2)}) %copy-start) | copy-done | bytes 196632
  2.2 0.0 copy-start.1
  2.2 0.9 %copy-done.1 = f32[3,8,16,128]{3,2,1,0:T(8,128)S(1)} copy-done((f32[3,8,16,128]{3,2,1,0:T(8,128)S(1)}, f32[3,8,16,128]{3,2,1,0:T(8,128)}, u32[]{:S(2)}) %copy-start.1) | copy-done | bytes 196632
  3.2 0.0 copy-start.2
  3.2 0.8 %copy-done.2 = s32[8,16,128]{2,1,0:T(8,128)S(1)} copy-done((s32[8,16,128]{2,1,0:T(8,128)S(1)}, s32[8,16,128]{2,1,0:T(8,128)}, u32[]{:S(2)}) %copy-start.2) | copy-done | bytes 65560
  4.0 0.0 copy-start.3
  4.0 0.8 %copy-done.3 = s32[8,16,128]{2,1,0:T(8,128)S(1)} copy-done((s32[8,16,128]{2,1,0:T(8,128)S(1)}, s32[8,16,128]{2,1,0:T(8,128)}, u32[]{:S(2)}) %copy-start.3) | copy-done | bytes 65560
  4.8 32.1 %shard_map.77 = (f32[3,8,16,128]{3,2,1,0:T(8,128)S(1)}, f32[1,4]{1,0:T(1,128)S(1)}) custom-call(f32[3,8,16,128]{3,2,1,0:T(8,128)S(1)} %copy-done, f32[3,8,16,128]{3,2,1,0:T(8,128)S(1)} %copy-done.1, s32[8,16,128]{2,1,0:T(8,128)S(1)} %copy-done.2, s32[8,16,128]{2,1,0:T(8,128)S(1)} %copy-done.3, s32[1,128]{1,0:T(1,128)S(1)} %bitcast.2, f32[4]{0:T(128)S(1)} %copy-done.5), custom_call_target="tpu_custom_call" | custom-call | flops 10000000 | bytes 1000000 | tf_op jit(solution)/shard_map/pallas_call | solution.py:389
  37.0 0.7 %copy.10 = f32[3,8,16,128]{3,2,1,0:T(8,128)} copy(f32[3,8,16,128]{3,2,1,0:T(8,128)S(1)} %get-tuple-element.8) | data formatting | bytes 393216
  37.6 0.5 %copy.11 = f32[4]{0:T(128)} copy(f32[4]{0:T(128)S(1)} %bitcast.3) | data formatting | bytes 32
Async XLA Ops:
  0.6 0.7 %copy-start.5 = (f32[4]{0:T(128)S(1)}, f32[4]{0:T(128)}, u32[]{:S(2)}) copy-start(f32[4]{0:T(128)} %mod_ref.1) | copy-start | bytes 52
  0.6 0.7 %copy-start.4 = (s32[128]{0:T(128)S(1)}, s32[128]{0:T(128)}, u32[]{:S(2)}) copy-start(s32[128]{0:T(128)} %param.10) | copy-start | bytes 1540
  1.3 0.9 %copy-start = (f32[3,8,16,128]{3,2,1,0:T(8,128)S(1)}, f32[3,8,16,128]{3,2,1,0:T(8,128)}, u32[]{:S(2)}) copy-start(f32[3,8,16,128]{3,2,1,0:T(8,128)} %disp.1) | copy-start | bytes 589828
  2.2 0.9 %copy-start.1 = (f32[3,8,16,128]{3,2,1,0:T(8,128)S(1)}, f32[3,8,16,128]{3,2,1,0:T(8,128)}, u32[]{:S(2)}) copy-start(f32[3,8,16,128]{3,2,1,0:T(8,128)} %load.1) | copy-start | bytes 589828
  3.2 0.8 %copy-start.2 = (s32[8,16,128]{2,1,0:T(8,128)S(1)}, s32[8,16,128]{2,1,0:T(8,128)}, u32[]{:S(2)}) copy-start(s32[8,16,128]{2,1,0:T(8,128)} %mask.1) | copy-start | bytes 196612
  4.0 0.8 %copy-start.3 = (s32[8,16,128]{2,1,0:T(8,128)S(1)}, s32[8,16,128]{2,1,0:T(8,128)}, u32[]{:S(2)}) copy-start(s32[8,16,128]{2,1,0:T(8,128)} %zone.1) | copy-start | bytes 196612

commit v2 on v1

--- a/solution.py
+++ b/solution.py
@@ -69,9 +69,10 @@
     return total
 
 
-def kernel(sizes, disp, load, mask, zone, slot_ref, mod_ref, adj_ref, grad_ref,
+def kernel(sizes, disp_in, load_in, mask_in, zone_in, slot_in, mod_in, adj_ref, grad_ref,
+           disp, load, mask, zone, slot_ref, mod_ref,
            E, BM, DM, NB, Q, QM, TB, G, MS, R, ZPL, ZPH, ZL, ZH, YPL, YPH, YL, YH,
-           ag_send, ag_recv, rs_send, rs_recv, hs, hr):
+           ag_send, ag_recv, rs_send, rs_recv, hs, hr, ins):
     nx, ny, nz = sizes
     n = nx * ny * nz
     cx, cy, cz = mask.shape
@@ -81,22 +82,36 @@
     ix, iy, iz = lax.axis_index("gx"), lax.axis_index("gy"), lax.axis_index("gz")
     me = (ix * ny + iy) * nz + iz
 
-    def place(t):
-        return (t // (ny * nz), (t // nz) % ny, t % nz)
+    barrier = pltpu.get_barrier_semaphore()
+    offsets = [(a, b, c) for a in range(nx) for b in range(ny) for c in range(nz)][1:]
+
+    def around(spot, step, count):
+        if step == 0:
+            return spot
+        there = spot + step
+        return jnp.where(there >= count, there - count, there)
+    xs = [around(ix, a, nx) for a in range(nx)]
+    ys = [around(iy, b, ny) for b in range(ny)]
+    zs = [around(iz, c, nz) for c in range(nz)]
+
+    def slot_at(a, b, c):
+        return ((-a % nx) * ny + (-b % ny)) * nz + (-c % nz) - 1
+
+    for a, b, c in offsets:
+        pl.semaphore_signal(barrier, inc=1, device_id=(xs[a], ys[b], zs[c]), device_id_type=MESH)
+    copies = [pltpu.make_async_copy(src, dst, ins.at[i]) for i, (src, dst) in enumerate(
+        ((mod_in, mod_ref), (load_in, load), (mask_in, mask), (zone_in, zone), (disp_in, disp),
+         (slot_in, slot_ref)))]
+    for copy in copies:
+        copy.start()
+    for copy in copies:
+        copy.wait()
 
     lane1 = lax.broadcasted_iota(jnp.int32, (1, 128), 1)
     row = jnp.zeros((1, 128), F32)
     for j in range(per):
         row = jnp.where(lane1 == (me * per) % 128 + j, mod_ref[j], row)
     G[me] = row
-
-    def send_mod(o, carry):
-        t = (me + o) % n
-        pltpu.make_async_remote_copy(
-            src_ref=G.at[me], dst_ref=G.at[me], send_sem=ag_send, recv_sem=ag_recv,
-            device_id=place(t), device_id_type=MESH).start()
-        return carry
-    lax.fori_loop(1, n, send_mod, 0)
 
     def exchange(axis, spot, count, low_src, high_dst, high_src, low_dst, s):
         down = pltpu.make_async_remote_copy(
@@ -156,6 +171,11 @@
     low, high = lax.fori_loop(0, cx, fill, (zero, zero))
     ZPL[...] = low
     ZPH[...] = high
+    pl.semaphore_wait(barrier, n - 1)
+    for a, b, c in offsets:
+        pltpu.make_async_remote_copy(
+            src_ref=G.at[me], dst_ref=G.at[me], send_sem=ag_send, recv_sem=ag_recv,
+            device_id=(xs[a], ys[b], zs[c]), device_id_type=MESH).start()
     exchange("gz", iz, nz, ZPL, ZH, ZPH, ZL, 0)
 
     def open_z(x, carry):
@@ -340,13 +360,12 @@
     MS[...] = jnp.zeros_like(MS)
     MS[:, 0, 0:16] = out
 
-    def send_sum(o, carry):
-        t = (me + o) % n
+    for a, b, c in offsets:
+        there = (xs[a], ys[b], zs[c])
+        t = (there[0] * ny + there[1]) * nz + there[2]
         pltpu.make_async_remote_copy(
-            src_ref=MS.at[t], dst_ref=R.at[n - 1 - o], send_sem=rs_send, recv_sem=rs_recv,
-            device_id=place(t), device_id_type=MESH).start()
-        return carry
-    lax.fori_loop(1, n, send_sum, 0)
+            src_ref=MS.at[t], dst_ref=R.at[slot_at(a, b, c)], send_sem=rs_send, recv_sem=rs_recv,
+            device_id=there, device_id_type=MESH).start()
     pltpu.make_async_copy(R, R, rs_recv).wait()
     pltpu.make_async_copy(R, R, rs_send).wait()
     row = jnp.sum(R[:, 0, :], axis=0, keepdims=True) + MS[me]
@@ -379,6 +398,7 @@
         per = zone_modulus.shape[0]
         wy, wz = cy + 8, 2 * cz
         vm = pl.BlockSpec(memory_space=pltpu.VMEM)
+        rows = zone_slot.shape[0] // 128
         scratch = [
             (8, cx + 3, wy, wz), (12, cx + 3, wy, wz), (12, cx + 1, cy, cz), (12, cx + 3, wy, wz),
             (3, cx + 1, cy, cz), (12, cx + 1, cy, cz), (2, cx + 2, cy, cz),
@@ -389,11 +409,15 @@
         adjoint, gradient = pl.pallas_call(
             functools.partial(kernel, sizes),
             out_shape=(jax.ShapeDtypeStruct(adjoint_load.shape, F32), jax.ShapeDtypeStruct((1, per), F32)),
-            in_specs=[vm] * 5 + [pl.BlockSpec(memory_space=pltpu.SMEM)],
+            in_specs=[pl.BlockSpec(memory_space=pltpu.HBM)] * 6,
             out_specs=(vm, vm),
-            scratch_shapes=[pltpu.VMEM(s, F32) for s in scratch]
-            + [pltpu.SemaphoreType.DMA] * 4 + [pltpu.SemaphoreType.DMA((6,))] * 2,
-            compiler_params=pltpu.CompilerParams(has_side_effects=True, vmem_limit_bytes=40 * 2**20),
+            scratch_shapes=[
+                pltpu.VMEM(displacement.shape, F32), pltpu.VMEM(adjoint_load.shape, F32),
+                pltpu.VMEM(bone_mask.shape, jnp.int32), pltpu.VMEM(elem_zone.shape, jnp.int32),
+                pltpu.VMEM((rows, 128), jnp.int32), pltpu.SMEM((per,), F32)]
+            + [pltpu.VMEM(s, F32) for s in scratch]
+            + [pltpu.SemaphoreType.DMA] * 4 + [pltpu.SemaphoreType.DMA((6,))] * 3,
+            compiler_params=pltpu.CompilerParams(collective_id=0, has_side_effects=True, vmem_limit_bytes=60 * 2**20),
             cost_estimate=pl.CostEstimate(flops=10**7, bytes_accessed=10**6, transcendentals=0),
         )(displacement, adjoint_load, bone_mask, elem_zone, zone_slot.reshape(-1, 128), zone_modulus)
         return adjoint, gradient.reshape(per)

time: 38.4 us -> 30 us (0.78)
  Pallas kernels: 32.1 us -> 27.1 us
  local copies, waits for them, and re-layouts: 5.38 us -> 2.13 us
    pallas_call x1, Pallas kernels: 32.1 us -> 27.1 us  [on_device(): pl.pallas_call(functools.partial(kernel, sizes), out_shape=(jax.ShapeDtyp...]
    unnamed x14 -> x4, local copies, waits for them, and re-layouts: 5.38 us -> 2.13 us
where the time goes in v2:
time: 30 us; the launch traced here: 29.9 us
  Pallas kernels  27.1 us (90%)
  local copies, waits for them, and re-layouts  2.13 us (7%)
  between operations  0.65 us (2%)
    pallas_call x1, Pallas kernels, on_device(): pl.pallas_call(functools.partial(kernel, sizes), out_shape=(jax.ShapeDtyp...  27.1 us
    unnamed x4, local copies, waits for them, and re-layouts  2.13 us

profile of v2, /device:TPU:0, one launch (start us, length us, event | category | flops | bytes accessed | tf_op | source)
XLA Modules:
  0.0 29.9 jit_solution(14782430557030490998)
XLA Ops:
  0.6 27.1 %shard_map.77 = (f32[3,8,16,128]{3,2,1,0:T(8,128)}, f32[1,4]{1,0:T(1,128)}) custom-call(f32[3,8,16,128]{3,2,1,0:T(8,128)} %disp_in.1, f32[3,8,16,128]{3,2,1,0:T(8,128)} %load_in.1, s32[8,16,128]{2,1,0:T(8,128)} %mask_in.1, s32[8,16,128]{2,1,0:T(8,128)} %zone_in.1, s32[1,128]{1,0:T(1,128)} %bitcast.2, f32[4]{0:T(128)} %mod_in.1), custom_call_target="tpu_custom_call" | custom-call | flops 10000000 | bytes 1000000 | tf_op jit(solution)/shard_map/pallas_call | solution.py:409
  27.7 0.0 copy-start
  27.7 1.6 %copy.10 = f32[3,8,16,128]{3,2,1,0:T(8,128)} copy(f32[3,8,16,128]{3,2,1,0:T(8,128)} %get-tuple-element.8) | data formatting | bytes 393216
  29.4 0.0 copy-done
  29.4 0.5 %copy.11 = f32[4]{0:T(128)} copy(f32[4]{0:T(128)S(1)} %bitcast.3) | data formatting | bytes 32
Async XLA Ops:
  27.7 1.6 %copy-start = (f32[1,4]{1,0:T(1,128)S(1)}, f32[1,4]{1,0:T(1,128)}, u32[]{:S(2)}) copy-start(f32[1,4]{1,0:T(1,128)} %get-tuple-element.5) | copy-start | bytes 52

commit v3 on v2

--- a/solution.py
+++ b/solution.py
@@ -113,39 +113,30 @@
         row = jnp.where(lane1 == (me * per) % 128 + j, mod_ref[j], row)
     G[me] = row
 
-    def exchange(axis, spot, count, low_src, high_dst, high_src, low_dst, s):
-        down = pltpu.make_async_remote_copy(
-            src_ref=low_src, dst_ref=high_dst, send_sem=hs.at[s], recv_sem=hr.at[s],
-            device_id={axis: jnp.maximum(spot - 1, 0)}, device_id_type=MESH)
-        up = pltpu.make_async_remote_copy(
-            src_ref=high_src, dst_ref=low_dst, send_sem=hs.at[s + 1], recv_sem=hr.at[s + 1],
-            device_id={axis: jnp.minimum(spot + 1, count - 1)}, device_id_type=MESH)
-
-        @pl.when(spot > 0)
-        def _():
-            down.start()
-
-        @pl.when(spot < count - 1)
-        def _():
-            up.start()
-
-        @pl.when(spot == 0)
-        def _():
-            low_dst[...] = jnp.zeros(low_dst.shape, F32)
-
-        @pl.when(spot == count - 1)
-        def _():
-            high_dst[...] = jnp.zeros(high_dst.shape, F32)
-
-        @pl.when(spot > 0)
-        def _():
-            down.wait_send()
-            up.wait_recv()
-
-        @pl.when(spot < count - 1)
-        def _():
-            up.wait_send()
-            down.wait_recv()
+    def remote(src, dst, send, recv, device):
+        return pltpu.make_async_remote_copy(
+            src_ref=src, dst_ref=dst, send_sem=hs.at[send], recv_sem=hr.at[recv],
+            device_id=device, device_id_type=MESH)
+
+    def links(entries):
+        for out, target, dst, _, source in entries:
+            pl.when(target)(out.start)
+
+            @pl.when(jnp.logical_not(source))
+            def _(dst=dst):
+                dst[...] = jnp.zeros(dst.shape, F32)
+
+        def finish():
+            for out, target, dst, sem, source in entries:
+                pl.when(target)(out.wait_send)
+                pl.when(source)(pltpu.make_async_copy(dst, dst, hr.at[sem]).wait)
+        return finish
+
+    def has(spot, step, count):
+        return jnp.logical_and(spot + step >= 0, spot + step < count)
+
+    def near(spot, step, count):
+        return jnp.clip(spot + step, 0, count - 1)
 
     lane = lax.broadcasted_iota(jnp.int32, (cy, 128), 1)
 
@@ -171,33 +162,52 @@
     low, high = lax.fori_loop(0, cx, fill, (zero, zero))
     ZPL[...] = low
     ZPH[...] = high
+    for f in range(8):
+        YPL[f] = E[f, 1:cx + 1, 0, 0:cz]
+        if f < 3:
+            YPL[8 + f] = E[f, 1:cx + 1, 1, 0:cz]
+        if f < LOW:
+            YPH[f] = E[f, 1:cx + 1, cy - 1, 0:cz]
     pl.semaphore_wait(barrier, n - 1)
+    entries = []
+    for d in (0, -1, 1):
+        for side, src, dst, step in ((0, ZPL, ZH, -1), (1, ZPH, ZL, 1)):
+            target = jnp.logical_and(has(iy, d, ny), has(iz, step, nz))
+            source = jnp.logical_and(has(iy, d, ny), has(iz, -step, nz))
+            out = remote(src, dst.at[1 - d], 3 * side + 1 + d, 3 * side + 1 - d,
+                         {"gy": near(iy, d, ny), "gz": near(iz, step, nz)})
+            entries.append((out, target, dst.at[1 + d], 3 * side + 1 + d, source))
+    for s, src, dst, step in ((6, YPL, YH, -1), (7, YPH, YL, 1)):
+        out = remote(src, dst, s, s, {"gy": near(iy, step, ny)})
+        entries.append((out, has(iy, step, ny), dst, s, has(iy, -step, ny)))
+    finish_zy = links(entries)
     for a, b, c in offsets:
         pltpu.make_async_remote_copy(
             src_ref=G.at[me], dst_ref=G.at[me], send_sem=ag_send, recv_sem=ag_recv,
             device_id=(xs[a], ys[b], zs[c]), device_id_type=MESH).start()
-    exchange("gz", iz, nz, ZPL, ZH, ZPH, ZL, 0)
+    for i in range(12):
+        NB[i, 1] = jnp.zeros((wy, wz), F32)
+    finish_zy()
+
+    line = lax.broadcasted_iota(jnp.int32, (8, 128), 0)
+    tall = lax.broadcasted_iota(jnp.int32, (wy, 128), 1)
+
+    def corners(ref):
+        return jnp.concatenate([ref[1], jnp.where(
+            line == 7, ref[0, cy - 8:cy], jnp.where(line < 2, ref[2, 0:8], 0.0))], axis=0)
+    above_z, below_z = corners(ZH), corners(ZL)
 
     def open_z(x, carry):
-        above, below = ZH[...], ZL[...]
+        above, below = carry
         for f in range(8):
-            tile = jnp.where(lane == 0, pltpu.roll(above, 128 - f * 8 - x, 1), 0.0)
+            tile = jnp.where(tall == 0, pltpu.roll(above, 128 - f * 8 - x, 1), 0.0)
             if f < 3:
-                tile = jnp.where(lane == 1, pltpu.roll(above, 128 + 1 - (8 + f) * 8 - x, 1), tile)
+                tile = jnp.where(tall == 1, pltpu.roll(above, 128 + 1 - (8 + f) * 8 - x, 1), tile)
             if f < LOW:
-                tile = jnp.where(lane == 127, pltpu.roll(below, 127 - f * 8 - x, 1), tile)
-            E[f, x + 1, 0:cy, cz:wz] = tile
+                tile = jnp.where(tall == 127, pltpu.roll(below, 127 - f * 8 - x, 1), tile)
+            E[f, x + 1, :, cz:wz] = tile
         return carry
-    lax.fori_loop(0, cx, open_z, 0)
-
-    for f in range(8):
-        YPL[f] = E[f, 1:cx + 1, 0, :]
-        if f < 3:
-            YPL[8 + f] = E[f, 1:cx + 1, 1, :]
-        if f < LOW:
-            YPH[f] = E[f, 1:cx + 1, cy - 1, :]
-    exchange("gy", iy, ny, YPL, YH, YPH, YL, 2)
-    line = lax.broadcasted_iota(jnp.int32, (8, wz), 0)
+    lax.fori_loop(0, cx, open_z, (above_z, below_z))
     for f in range(8):
         above = YH[f]
         second = YH[8 + f] if f < 3 else None
@@ -208,9 +218,43 @@
                 tile = jnp.where(line == 1, second[x:x + 1], tile)
             if f < LOW:
                 tile = jnp.where(line == 7, below[x:x + 1], tile)
-            E[f, x + 1, cy:wy, :] = tile
-    exchange("gx", ix, nx, E.at[:, pl.ds(1, 2)], E.at[:, pl.ds(cx + 1, 2)],
-             E.at[pl.ds(0, LOW), pl.ds(cx, 1)], E.at[pl.ds(0, LOW), pl.ds(0, 1)], 4)
+            E[f, x + 1, cy:wy, 0:cz] = tile
+    finish_x = links([
+        (remote(E.at[:, pl.ds(1, 2)], E.at[:, pl.ds(cx + 1, 2)], 8, 8, {"gx": near(ix, -1, nx)}),
+         has(ix, -1, nx), E.at[:, pl.ds(cx + 1, 2)], 8, has(ix, 1, nx)),
+        (remote(E.at[pl.ds(0, LOW), pl.ds(cx, 1)], E.at[pl.ds(0, LOW), pl.ds(0, 1)], 9, 9,
+                {"gx": near(ix, 1, nx)}),
+         has(ix, 1, nx), E.at[pl.ds(0, LOW), pl.ds(0, 1)], 9, has(ix, -1, nx)),
+    ])
+
+    def yz_modes(v, put, x, k):
+        after = pltpu.roll(v, wz - 1, 1)
+        for c, t in enumerate((v + after, after - v)):
+            above = pltpu.roll(t, wy - 1, 0)
+            put(4 * k + c, x, t + above)
+            put(4 * k + 2 + c, x, above - t)
+
+    def put_b(i, x, v):
+        BM[i, x] = v
+
+    def put_d(i, x, v):
+        DM[i, x] = v[0:cy, 0:cz]
+
+    def put_q(i, x, v):
+        QM[i, x] = v[0:cy, 0:cz]
+
+    def b_modes(x, carry):
+        for k in range(3):
+            yz_modes(E[k, x], put_b, x, k)
+        return carry
+
+    def d_modes(x, carry):
+        for k in range(3):
+            yz_modes(E[5 + k, x + 1], put_d, x, k)
+        return carry
+
+    lax.fori_loop(0, cx, d_modes, 0)
+    lax.fori_loop(1, cx + 1, b_modes, 0)
 
     whole = G.at[pl.ds(0, n - 1)]
     pltpu.make_async_copy(whole, whole, ag_recv).wait()
@@ -231,35 +275,7 @@
         index = jnp.broadcast_to(slot_ref[g:g + 1, :], (8, 128))
         by_zone.append(look_up(by_slot, index)[0:1])
 
-    def yz_modes(v, put, x, k):
-        after = pltpu.roll(v, wz - 1, 1)
-        for c, t in enumerate((v + after, after - v)):
-            above = pltpu.roll(t, wy - 1, 0)
-            put(4 * k + c, x, t + above)
-            put(4 * k + 2 + c, x, above - t)
-
-    def put_b(i, x, v):
-        BM[i, x] = v
-
-    def put_d(i, x, v):
-        DM[i, x] = v[0:cy, 0:cz]
-
-    def put_q(i, x, v):
-        QM[i, x] = v[0:cy, 0:cz]
-
-    def b_modes(x, carry):
-        for k in range(3):
-            yz_modes(E[k, x], put_b, x, k)
-        return carry
-    lax.fori_loop(0, cx + 3, b_modes, 0)
-
-    def d_modes(x, carry):
-        for k in range(3):
-            yz_modes(E[5 + k, x + 1], put_d, x, k)
-        return carry
-    lax.fori_loop(0, cx + 1, d_modes, 0)
-
-    def first(x, carry):
+    def first(x, carry, lowest=False):
         where = E[4, x].astype(jnp.int32)
         parts = []
         for y in range(0, wy, 8):
@@ -269,10 +285,11 @@
         TB[1, x] = stiff[0:cy, 0:cz]
         f = element_forces(modes_of(lambda i, p: BM[i, p], x))
 
-        @pl.when(jnp.logical_and(x > 0, x <= cx))
-        def _():
+        def terms():
             inner = [[[[None if t is None else t[0:cy, 0:cz] for t in b] for b in a] for a in k] for k in f]
             TB[0, x] = dot_modes(inner, modes_of(lambda i, p: DM[i, p], x - 1))
+        if not lowest:
+            pl.when(x <= cx)(terms)
         for k in range(3):
             for b in range(2):
                 for c in range(2):
@@ -283,12 +300,19 @@
                         now, later = total - delta, total + delta
                     else:
                         now, later = -delta, delta
-                    NB[i, x] = NB[i, x] + now
-                    NB[i, x + 1] = later
+                    if lowest:
+                        NB[i, 1] = NB[i, 1] + later
+                    else:
+                        NB[i, x] = NB[i, x] + now
+                        NB[i, x + 1] = later
         return carry
-    for i in range(12):
-        NB[i, 0] = jnp.zeros((wy, wz), F32)
-    lax.fori_loop(0, cx + 2, first, 0)
+    lax.fori_loop(1, cx, first, 0)
+    finish_x()
+    b_modes(0, 0)
+    lax.fori_loop(cx + 1, cx + 3, b_modes, 0)
+    d_modes(cx, 0)
+    lax.fori_loop(cx, cx + 2, first, 0)
+    first(0, 0, lowest=True)
 
     at_y = lax.broadcasted_iota(jnp.int32, (wy, wz), 0)
     at_z = lax.broadcasted_iota(jnp.int32, (wy, wz), 1)
@@ -403,8 +427,8 @@
             (8, cx + 3, wy, wz), (12, cx + 3, wy, wz), (12, cx + 1, cy, cz), (12, cx + 3, wy, wz),
             (3, cx + 1, cy, cz), (12, cx + 1, cy, cz), (2, cx + 2, cy, cz),
             (n, 1, 128), (n, 1, 128), (n - 1, 1, 128),
-            (cy, 128), (cy, 128), (cy, 128), (cy, 128),
-            (11, cx, wz), (LOW, cx, wz), (LOW, cx, wz), (11, cx, wz),
+            (cy, 128), (cy, 128), (3, cy, 128), (3, cy, 128),
+            (11, cx, cz), (LOW, cx, cz), (LOW, cx, cz), (11, cx, cz),
         ]
         adjoint, gradient = pl.pallas_call(
             functools.partial(kernel, sizes),
@@ -416,7 +440,7 @@
                 pltpu.VMEM(bone_mask.shape, jnp.int32), pltpu.VMEM(elem_zone.shape, jnp.int32),
                 pltpu.VMEM((rows, 128), jnp.int32), pltpu.SMEM((per,), F32)]
             + [pltpu.VMEM(s, F32) for s in scratch]
-            + [pltpu.SemaphoreType.DMA] * 4 + [pltpu.SemaphoreType.DMA((6,))] * 3,
+            + [pltpu.SemaphoreType.DMA] * 4 + [pltpu.SemaphoreType.DMA((10,))] * 2 + [pltpu.SemaphoreType.DMA((6,))],
             compiler_params=pltpu.CompilerParams(collective_id=0, has_side_effects=True, vmem_limit_bytes=60 * 2**20),
             cost_estimate=pl.CostEstimate(flops=10**7, bytes_accessed=10**6, transcendentals=0),
         )(displacement, adjoint_load, bone_mask, elem_zone, zone_slot.reshape(-1, 128), zone_modulus)

time: 30 us -> 25.9 us (0.86)
  Pallas kernels: 27.1 us -> 22.9 us
    pallas_call x1, Pallas kernels: 27.1 us -> 22.9 us  [on_device(): pl.pallas_call(functools.partial(kernel, sizes), out_shape=(jax.ShapeDtyp...]
where the time goes in v3:
time: 25.9 us; the launch traced here: 25.7 us
  Pallas kernels  22.9 us (88%)
  local copies, waits for them, and re-layouts  2.13 us (8%)
  between operations  0.65 us (3%)
    pallas_call x1, Pallas kernels, on_device(): pl.pallas_call(functools.partial(kernel, sizes), out_shape=(jax.ShapeDtyp...  22.9 us
    unnamed x4, local copies, waits for them, and re-layouts  2.13 us

profile of v3, /device:TPU:0, one launch (start us, length us, event | category | flops | bytes accessed | tf_op | source)
XLA Modules:
  0.0 25.7 jit_solution(2153264491811340191)
XLA Ops:
  0.6 22.9 %shard_map.77 = (f32[3,8,16,128]{3,2,1,0:T(8,128)}, f32[1,4]{1,0:T(1,128)}) custom-call(f32[3,8,16,128]{3,2,1,0:T(8,128)} %disp_in.1, f32[3,8,16,128]{3,2,1,0:T(8,128)} %load_in.1, s32[8,16,128]{2,1,0:T(8,128)} %mask_in.1, s32[8,16,128]{2,1,0:T(8,128)} %zone_in.1, s32[1,128]{1,0:T(1,128)} %bitcast.2, f32[4]{0:T(128)} %mod_in.1), custom_call_target="tpu_custom_call" | custom-call | flops 10000000 | bytes 1000000 | tf_op jit(solution)/shard_map/pallas_call | solution.py:433
  23.6 0.0 copy-start
  23.6 1.6 %copy.10 = f32[3,8,16,128]{3,2,1,0:T(8,128)} copy(f32[3,8,16,128]{3,2,1,0:T(8,128)} %get-tuple-element.8) | data formatting | bytes 393216
  25.2 0.0 copy-done
  25.2 0.5 %copy.11 = f32[4]{0:T(128)} copy(f32[4]{0:T(128)S(1)} %bitcast.3) | data formatting | bytes 32
Async XLA Ops:
  23.6 1.6 %copy-start = (f32[1,4]{1,0:T(1,128)S(1)}, f32[1,4]{1,0:T(1,128)}, u32[]{:S(2)}) copy-start(f32[1,4]{1,0:T(1,128)} %get-tuple-element.5) | copy-start | bytes 52

commit v4 on v3

--- a/solution.py
+++ b/solution.py
@@ -441,9 +441,10 @@
                 pltpu.VMEM((rows, 128), jnp.int32), pltpu.SMEM((per,), F32)]
             + [pltpu.VMEM(s, F32) for s in scratch]
             + [pltpu.SemaphoreType.DMA] * 4 + [pltpu.SemaphoreType.DMA((10,))] * 2 + [pltpu.SemaphoreType.DMA((6,))],
-            compiler_params=pltpu.CompilerParams(collective_id=0, has_side_effects=True, vmem_limit_bytes=60 * 2**20),
+            compiler_params=pltpu.CompilerParams(collective_id=0, has_side_effects=True, vmem_limit_bytes=40 * 2**20),
             cost_estimate=pl.CostEstimate(flops=10**7, bytes_accessed=10**6, transcendentals=0),
-        )(displacement, adjoint_load, bone_mask, elem_zone, zone_slot.reshape(-1, 128), zone_modulus)
+        )(*[pltpu.with_memory_space_constraint(v, pltpu.HBM) for v in (
+            displacement, adjoint_load, bone_mask, elem_zone, zone_slot.reshape(-1, 128), zone_modulus)])
         return adjoint, gradient.reshape(per)
 
     whole = P(None, "gx", "gy", "gz")

time: 25.9 us -> 24.3 us (0.938)
  local copies, waits for them, and re-layouts: 2.13 us -> 1.19 us
  Pallas kernels: 22.9 us -> 22.3 us
    unnamed x4 -> x2, local copies, waits for them, and re-layouts: 2.13 us -> 1.19 us
    pallas_call x1, Pallas kernels: 22.9 us -> 22.3 us  [on_device(): pl.pallas_call(functools.partial(kernel, sizes), out_shape=(jax.ShapeDtyp...]
where the time goes in v4:
time: 24.3 us; the launch traced here: 24.1 us
  Pallas kernels  22.3 us (92%)
  local copies, waits for them, and re-layouts  1.19 us (5%)
  between operations  0.64 us (3%)
    pallas_call x1, Pallas kernels, on_device(): pl.pallas_call(functools.partial(kernel, sizes), out_shape=(jax.ShapeDtyp...  22.3 us
    unnamed x2, local copies, waits for them, and re-layouts  1.19 us

profile of v4, /device:TPU:0, one launch (start us, length us, event | category | flops | bytes accessed | tf_op | source)
XLA Modules:
  0.0 24.1 jit_solution(10619964779631264491)
XLA Ops:
  0.6 22.3 %shard_map.77 = (f32[3,8,16,128]{3,2,1,0:T(8,128)S(1)}, f32[1,4]{1,0:T(1,128)S(1)}) custom-call(f32[3,8,16,128]{3,2,1,0:T(8,128)} %disp_in.1, f32[3,8,16,128]{3,2,1,0:T(8,128)} %load_in.1, s32[8,16,128]{2,1,0:T(8,128)} %mask_in.1, s32[8,16,128]{2,1,0:T(8,128)} %zone_in.1, s32[1,128]{1,0:T(1,128)} %bitcast.3, f32[4]{0:T(128)} %mod_in.1), custom_call_target="tpu_custom_call" | custom-call | flops 10000000 | bytes 1000000 | tf_op jit(solution)/shard_map/pallas_call | solution.py:433
  22.9 0.7 %copy.10 = f32[3,8,16,128]{3,2,1,0:T(8,128)} copy(f32[3,8,16,128]{3,2,1,0:T(8,128)S(1)} %get-tuple-element.8) | data formatting | bytes 393216
  23.6 0.5 %copy.11 = f32[4]{0:T(128)} copy(f32[4]{0:T(128)S(1)} %bitcast.2) | data formatting | bytes 32

commit v5 on v4

--- a/solution.py
+++ b/solution.py
@@ -159,7 +159,7 @@
                 high = jnp.where(lane == f * 8 + x, pltpu.roll(value, f * 8 + x + 1, 1), high)
         return low, high
     zero = jnp.zeros((cy, 128), F32)
-    low, high = lax.fori_loop(0, cx, fill, (zero, zero))
+    low, high = lax.fori_loop(0, cx, fill, (zero, zero), unroll=True)
     ZPL[...] = low
     ZPH[...] = high
     for f in range(8):
@@ -207,7 +207,7 @@
                 tile = jnp.where(tall == 127, pltpu.roll(below, 127 - f * 8 - x, 1), tile)
             E[f, x + 1, :, cz:wz] = tile
         return carry
-    lax.fori_loop(0, cx, open_z, (above_z, below_z))
+    lax.fori_loop(0, cx, open_z, (above_z, below_z), unroll=True)
     for f in range(8):
         above = YH[f]
         second = YH[8 + f] if f < 3 else None
@@ -253,12 +253,11 @@
             yz_modes(E[5 + k, x + 1], put_d, x, k)
         return carry
 
-    lax.fori_loop(0, cx, d_modes, 0)
-    lax.fori_loop(1, cx + 1, b_modes, 0)
+    lax.fori_loop(0, cx, d_modes, 0, unroll=True)
+    lax.fori_loop(1, cx + 1, b_modes, 0, unroll=True)
 
     whole = G.at[pl.ds(0, n - 1)]
     pltpu.make_async_copy(whole, whole, ag_recv).wait()
-    pltpu.make_async_copy(whole, whole, ag_send).wait()
     group = n // rows
     by_slot = [jnp.sum(G[g * group:(g + 1) * group, 0, :], axis=0, keepdims=True) for g in range(rows)]
 
@@ -341,7 +340,7 @@
             bb = bb + own * (v * v)
             yz_modes(q, put_q, x, k)
         return bq, qq, bb
-    bq, qq, bb = lax.fori_loop(0, cx + 1, nodes, (zero, zero, zero))
+    bq, qq, bb = lax.fori_loop(0, cx + 1, nodes, (zero, zero, zero), unroll=True)
 
     scale = -(ZS ** -1.5)
     first_zone = zone[0]
@@ -360,7 +359,7 @@
         b1 = b1 + jnp.where(same, 0.0, t1)
         b2 = b2 + jnp.where(same, 0.0, t2)
         return energy, a1, a2, b1, b2
-    energy, a1, a2, b1, b2 = lax.fori_loop(0, cx, second, (zero,) * 5)
+    energy, a1, a2, b1, b2 = lax.fori_loop(0, cx, second, (zero,) * 5, unroll=True)
 
     owner = lax.broadcasted_iota(jnp.int32, (n, 128), 0)
     sub = lax.broadcasted_iota(jnp.int32, (16, 128), 0)
@@ -391,7 +390,6 @@
             src_ref=MS.at[t], dst_ref=R.at[slot_at(a, b, c)], send_sem=rs_send, recv_sem=rs_recv,
             device_id=there, device_id_type=MESH).start()
     pltpu.make_async_copy(R, R, rs_recv).wait()
-    pltpu.make_async_copy(R, R, rs_send).wait()
     row = jnp.sum(R[:, 0, :], axis=0, keepdims=True) + MS[me]
 
     def pick(j):
@@ -410,7 +408,9 @@
         for k in range(3):
             adj_ref[k, x] = c1 * load[k, x] + c2 * Q[k, x]
         return carry
-    lax.fori_loop(0, cx, finish, 0)
+    lax.fori_loop(0, cx, finish, 0, unroll=True)
+    pltpu.make_async_copy(whole, whole, ag_send).wait()
+    pltpu.make_async_copy(R, R, rs_send).wait()
 
 
 def solution(mesh):

time: 24.3 us -> 22.4 us (0.922)
  Pallas kernels: 22.3 us -> 20.4 us
    pallas_call x1, Pallas kernels: 22.3 us -> 20.4 us  [on_device(): pl.pallas_call(functools.partial(kernel, sizes), out_shape=(jax.ShapeDtyp...]
where the time goes in v5:
time: 22.4 us; the launch traced here: 22.2 us
  Pallas kernels  20.4 us (91%)
  local copies, waits for them, and re-layouts  1.19 us (5%)
  between operations  0.64 us (3%)
    pallas_call x1, Pallas kernels, on_device(): pl.pallas_call(functools.partial(kernel, sizes), out_shape=(jax.ShapeDtyp...  20.4 us
    unnamed x2, local copies, waits for them, and re-layouts  1.19 us

profile of v5, /device:TPU:0, one launch (start us, length us, event | category | flops | bytes accessed | tf_op | source)
XLA Modules:
  0.0 22.2 jit_solution(613932962426549148)
XLA Ops:
  0.6 20.4 %shard_map.77 = (f32[3,8,16,128]{3,2,1,0:T(8,128)S(1)}, f32[1,4]{1,0:T(1,128)S(1)}) custom-call(f32[3,8,16,128]{3,2,1,0:T(8,128)} %disp_in.1, f32[3,8,16,128]{3,2,1,0:T(8,128)} %load_in.1, s32[8,16,128]{2,1,0:T(8,128)} %mask_in.1, s32[8,16,128]{2,1,0:T(8,128)} %zone_in.1, s32[1,128]{1,0:T(1,128)} %bitcast.3, f32[4]{0:T(128)} %mod_in.1), custom_call_target="tpu_custom_call" | custom-call | flops 10000000 | bytes 1000000 | tf_op jit(solution)/shard_map/pallas_call | solution.py:433
  21.0 0.7 %copy.10 = f32[3,8,16,128]{3,2,1,0:T(8,128)} copy(f32[3,8,16,128]{3,2,1,0:T(8,128)S(1)} %get-tuple-element.8) | data formatting | bytes 393216
  21.7 0.5 %copy.11 = f32[4]{0:T(128)} copy(f32[4]{0:T(128)S(1)} %bitcast.2) | data formatting | bytes 32

commit v6 on v5

--- a/solution.py
+++ b/solution.py
@@ -305,12 +305,12 @@
                         NB[i, x] = NB[i, x] + now
                         NB[i, x + 1] = later
         return carry
-    lax.fori_loop(1, cx, first, 0)
+    lax.fori_loop(1, cx, first, 0, unroll=True)
     finish_x()
     b_modes(0, 0)
-    lax.fori_loop(cx + 1, cx + 3, b_modes, 0)
+    lax.fori_loop(cx + 1, cx + 3, b_modes, 0, unroll=True)
     d_modes(cx, 0)
-    lax.fori_loop(cx, cx + 2, first, 0)
+    lax.fori_loop(cx, cx + 2, first, 0, unroll=True)
     first(0, 0, lowest=True)
 
     at_y = lax.broadcasted_iota(jnp.int32, (wy, wz), 0)

time: 22.4 us -> 21.2 us (0.946)
  Pallas kernels: 20.4 us -> 19.2 us
    pallas_call x1, Pallas kernels: 20.4 us -> 19.2 us  [on_device(): pl.pallas_call(functools.partial(kernel, sizes), out_shape=(jax.ShapeDtyp...]
where the time goes in v6:
time: 21.2 us; the launch traced here: 21 us
  Pallas kernels  19.2 us (91%)
  local copies, waits for them, and re-layouts  1.19 us (6%)
  between operations  0.64 us (3%)
    pallas_call x1, Pallas kernels, on_device(): pl.pallas_call(functools.partial(kernel, sizes), out_shape=(jax.ShapeDtyp...  19.2 us
    unnamed x2, local copies, waits for them, and re-layouts  1.19 us

profile of v6, /device:TPU:0, one launch (start us, length us, event | category | flops | bytes accessed | tf_op | source)
XLA Modules:
  0.0 21.0 jit_solution(17649270350660174647)
XLA Ops:
  0.6 19.2 %shard_map.77 = (f32[3,8,16,128]{3,2,1,0:T(8,128)S(1)}, f32[1,4]{1,0:T(1,128)S(1)}) custom-call(f32[3,8,16,128]{3,2,1,0:T(8,128)} %disp_in.1, f32[3,8,16,128]{3,2,1,0:T(8,128)} %load_in.1, s32[8,16,128]{2,1,0:T(8,128)} %mask_in.1, s32[8,16,128]{2,1,0:T(8,128)} %zone_in.1, s32[1,128]{1,0:T(1,128)} %bitcast.3, f32[4]{0:T(128)} %mod_in.1), custom_call_target="tpu_custom_call" | custom-call | flops 10000000 | bytes 1000000 | tf_op jit(solution)/shard_map/pallas_call | solution.py:433
  19.8 0.7 %copy.10 = f32[3,8,16,128]{3,2,1,0:T(8,128)} copy(f32[3,8,16,128]{3,2,1,0:T(8,128)S(1)} %get-tuple-element.8) | data formatting | bytes 393216
  20.5 0.5 %copy.11 = f32[4]{0:T(128)} copy(f32[4]{0:T(128)S(1)} %bitcast.2) | data formatting | bytes 32
